TPU v7x, 32 devices: a whole 2x2x4 slice. The times are simulated.
32 devices in a mesh: replica: 8 (over y, x, core), fsdp: 4 (over z).
Axes of the slice: x: 2, y: 2, z: 4, core: 2. Of those that a mesh axis runs over, the one named last changes fastest.
Arguments:
- inputs: bfloat16 [2, 4096, 4096], P(None, ('replica', 'fsdp')), may hold values from -6 to 6
- cotangents: bfloat16 [2, 4096, 512], P(None, ('replica', 'fsdp')), may hold values from -1.0546875 to 1.0546875
- weights: float32 [8, 4096, 512], P('replica', 'fsdp'), may hold values from -6 to 6
- first_moment: bfloat16 [8, 4096, 512], P('replica', 'fsdp'), may hold values from -6 to 6
- second_moment: bfloat16 [8, 4096, 512], P('replica', 'fsdp'), may hold values from 0.5 to 8
- anchor: float32 [4096, 512], P('fsdp'), may hold values from -6 to 6
- outer_momentum: float32 [4096, 512], P('fsdp'), may hold values from -3 to 3
Outputs:
- weights_out: float32 [8, 4096, 512], P('replica', 'fsdp')
- first_out: bfloat16 [8, 4096, 512], P('replica', 'fsdp')
- second_out: bfloat16 [8, 4096, 512], P('replica', 'fsdp')
- anchor_out: float32 [4096, 512], P('fsdp')
- momentum_out: float32 [4096, 512], P('fsdp')
All inputs are finite; a program needn't handle non-finite values.
Results may differ from a plain program's by a relative error of at most 0.008.
Values may be sent and summed in bfloat16 or wider, within the bound.
A program may use at most 64 MiB of HBM per device.

v0:
```python
import jax
import jax.numpy as jnp
from jax import lax
from jax.sharding import PartitionSpec as P

BETA_FIRST = 0.9
BETA_SECOND = 0.95
INNER_RATE = 0.01
WEIGHT_DECAY = 0.1
EPSILON = 1e-08
OUTER_RATE = 0.7
MOMENTUM_KEEP = 0.9
MERGE_WEIGHT = 0.5


def inner_update(weight, first_moment, second_moment, gradient):
    first_new = (
        BETA_FIRST * first_moment.astype(jnp.float32) + (1.0 - BETA_FIRST) * gradient
    ).astype(jnp.bfloat16)
    second_new = (
        BETA_SECOND * second_moment.astype(jnp.float32) + (1.0 - BETA_SECOND) * gradient * gradient
    ).astype(jnp.bfloat16)
    first_kept, second_kept = lax.optimization_barrier((first_new, second_new))
    first_read = first_kept.astype(jnp.float32)
    second_read = second_kept.astype(jnp.float32)
    weight_new = weight - INNER_RATE * (
        first_read / (jnp.sqrt(second_read) + EPSILON) + WEIGHT_DECAY * weight
    )
    return (weight_new, first_new, second_new)


def fold_columns(columns, piece):
    return jnp.einsum("std,stf->sdf", columns, piece, preferred_element_type=jnp.float32)


def body(inputs, cotangents, weights, first_moment, second_moment, anchor, outer_momentum):
    step_count = inputs.shape[0]
    drift = anchor - weights[0]
    summed = lax.psum(drift, "replica")
    pseudo = summed / lax.axis_size("replica")
    momentum_out = MOMENTUM_KEEP * outer_momentum + pseudo
    anchor_out = anchor - OUTER_RATE * (pseudo + MOMENTUM_KEEP * momentum_out)
    gradients = []
    for which in range(step_count):
        columns = lax.all_to_all(
            inputs[which : which + 1], "fsdp", split_axis=2, concat_axis=1, tiled=True
        )
        folded = fold_columns(
            columns, lax.all_gather(cotangents[which : which + 1], "fsdp", axis=1, tiled=True)
        )
        gradients.append(folded[0])
    weight = weights[0]
    first_state = first_moment[0]
    second_state = second_moment[0]
    for which in range(step_count):
        weight, first_state, second_state = inner_update(
            weight, first_state, second_state, gradients[which]
        )
        if which == 0:
            weight = MERGE_WEIGHT * weight + (1.0 - MERGE_WEIGHT) * anchor_out
    return (weight[None], first_state[None], second_state[None], anchor_out, momentum_out)


def solution(mesh):
    in_specs = (
        P(None, ("replica", "fsdp"), None),
        P(None, ("replica", "fsdp"), None),
        P("replica", "fsdp", None),
        P("replica", "fsdp", None),
        P("replica", "fsdp", None),
        P("fsdp", None),
        P("fsdp", None),
    )
    out_specs = (
        P("replica", "fsdp", None),
        P("replica", "fsdp", None),
        P("replica", "fsdp", None),
        P("fsdp", None),
        P("fsdp", None),
    )
    return jax.shard_map(body, mesh=mesh, in_specs=in_specs, out_specs=out_specs, check_vma=False)
```

profile of v0, /device:TPU:0, one launch (start us, length us, event | category | flops | bytes accessed | tf_op | source)
XLA Modules:
  0.0 168.3 jit_solution(18412162903958992177)
XLA Ops:
  7.2 2.7 %fusion.14 = (bf16[1,128,4096]{2,1,0:T(8,128)(2,1)S(1)}, bf16[1,128,4096]{2,1,0:T(8,128)(2,1)}) fusion(bf16[2,128,4096]{2,1,0:T(8,128)(2,1)} %param.7), kind=kLoop, calls=%fused_computation.22 | loop fusion | bytes 4194304 | tf_op jit(solution)/shard_map/slice | solution.py:46
  9.9 2.8 %copy.22 = bf16[1,128,4096]{1,0,2:T(2,128)(2,1)S(1)} copy(bf16[1,128,4096]{2,1,0:T(8,128)(2,1)S(1)} %get-tuple-element.22) | data formatting | bytes 2097152
  12.7 0.5 broadcast.61
  13.2 22.4 %reduce = bf16[4096,128]{1,0:T(8,128)(2,1)S(1)} reduce(bf16[4096,1,128]{2,1,0:T(2,128)(2,1)S(1)} %bitcast.50, bf16[]{:T(256)} %broadcast.61), dimensions={1}, to_apply=%bitcast.40.reduce_sub_computation | reduce | bytes 2097154
  35.6 1.7 reshape.40
  37.2 6.3 %all-to-all-start = ((bf16[4,2,65536]{2,1,0:T(2,128)(2,1)}), bf16[4,2,65536]{2,1,0:T(2,128)(2,1)S(1)}, u32[]{:S(2)}, u32[]{:S(2)}) async-start(bf16[4,2,65536]{2,1,0:T(2,128)(2,1)} %reshape.40), calls=%async_computation | async-start | bytes 2097152 | tf_op jit(solution)/shard_map/all_to_all | solution.py:45
  43.5 5.0 %copy.23 = bf16[1,128,4096]{1,0,2:T(2,128)(2,1)S(1)} copy(bf16[1,128,4096]{2,1,0:T(8,128)(2,1)} %get-tuple-element.23) | data formatting | bytes 2097152
  48.6 23.4 %reduce.1 = bf16[4096,128]{1,0:T(8,128)(2,1)} reduce(bf16[4096,1,128]{2,1,0:T(2,128)(2,1)S(1)} %bitcast.51, bf16[]{:T(256)} %broadcast.61), dimensions={1}, to_apply=%bitcast.38.reduce_sub_computation | reduce | bytes 2097154
  71.9 3.6 %reshape.38 = bf16[4,2,65536]{2,1,0:T(2,128)(2,1)} reshape(bf16[4096,128]{1,0:T(8,128)(2,1)} %reduce.1) | data formatting | bytes 2097152
  75.6 0.0 all-to-all-done
  75.6 5.1 %all-to-all-start.1 = ((bf16[4,2,65536]{2,1,0:T(2,128)(2,1)}), bf16[4,2,65536]{2,1,0:T(2,128)(2,1)}, u32[]{:S(2)}, u32[]{:S(2)}) async-start(bf16[4,2,65536]{2,1,0:T(2,128)(2,1)} %reshape.38), calls=%async_computation.1 | async-start | bytes 2097152 | tf_op jit(solution)/shard_map/all_to_all | solution.py:45
  80.7 0.0 all-reduce.2.cloned.1.call-start
  80.7 0.0 copy-done
  80.7 3.4 %bitcast_subtract_fusion = f32[1024,512]{1,0:T(8,128)} fusion(f32[1024,512]{1,0:T(8,128)} %param.12, f32[1,1024,512]{2,1,0:T(8,128)S(1)} %copy-done), kind=kLoop, calls=%fused_computation.8 | loop fusion | flops 524288 | bytes 6291456 | tf_op jit(solution)/shard_map/sub | solution.py:38
  84.1 0.0 all-reduce.2.cloned.1.call-update
  84.1 0.9 copy-done.4
  85.0 31.5 %all_gather.6 = bf16[1,512,512]{2,1,0:T(8,128)(2,1)} all-gather(bf16[1,128,512]{2,1,0:T(8,128)(2,1)S(1)} %get-tuple-element.24), channel_id=1, replica_groups=mesh['replica'=8,'fsdp'=4] {'fsdp'}, dimensions={1}, use_global_device_ids=true | all-gather | bytes 655360 | tf_op jit(solution)/shard_map/all_gather | solution.py:49
  116.5 16.9 %all_gather.7 = bf16[1,512,512]{2,1,0:T(8,128)(2,1)} all-gather(bf16[1,128,512]{2,1,0:T(8,128)(2,1)S(1)} %get-tuple-element.25), channel_id=1, replica_groups=mesh['replica'=8,'fsdp'=4] {'fsdp'}, dimensions={1}, use_global_device_ids=true | all-gather | bytes 655360 | tf_op jit(solution)/shard_map/all_gather | solution.py:49
  133.4 2.3 %reshape.41 = bf16[4096,1,128]{2,1,0:T(2,128)(2,1)} reshape(bf16[4,2,65536]{2,1,0:T(2,128)(2,1)S(1)} %all-to-all-done) | data formatting | bytes 2097152
  135.7 2.8 %copy.20 = bf16[1,128,4096]{1,2,0:T(8,128)(2,1)} copy(bf16[1,128,4096]{1,0,2:T(2,128)(2,1)} %bitcast.48) | data formatting | bytes 2097152
  138.5 1.5 copy.17
  140.0 0.0 all-to-all-done.1
  140.0 4.0 %reshape.39 = bf16[4096,1,128]{2,1,0:T(2,128)(2,1)} reshape(bf16[4,2,65536]{2,1,0:T(2,128)(2,1)} %all-to-all-done.1) | data formatting | bytes 2097152
  144.0 2.7 %copy.21 = bf16[1,128,4096]{1,2,0:T(8,128)(2,1)} copy(bf16[1,128,4096]{1,0,2:T(2,128)(2,1)} %bitcast.49) | data formatting | bytes 2097152
  146.7 2.3 %copy.19 = bf16[1,4,128,1024]{3,2,1,0:T(8,128)(2,1)} copy(bf16[1,4,128,1024]{2,3,1,0:T(8,128)(2,1)} %bitcast.54) | data formatting | bytes 2097152 | tf_op jit(solution)/shard_map/all_to_all | solution.py:45
  149.0 1.9 %fusion.10 = f32[1024,512]{1,0:T(8,128)S(1)} fusion(bf16[512,1024]{1,0:T(8,128)(2,1)S(1)} %bitcast.52, bf16[1,512,512]{2,1,0:T(8,128)(2,1)} %all_gather.6), kind=kOutput, calls=%fused_computation.20 | convolution fusion | flops 536870912 | bytes 3670016 | tf_op jit(solution)/shard_map/std,stf->sdf/dot_general | solution.py:33
  150.9 0.0 copy-done.2
  150.9 0.0 copy-done.3
  150.9 0.0 copy-done.5
  150.9 0.2 copy-done.6
  151.1 3.3 %fusion.3 = (bf16[1024,512]{1,0:T(8,128)(2,1)S(1)}, bf16[1024,512]{1,0:T(8,128)(2,1)}, bf16[1024,512]{1,0:T(8,128)(2,1)}, bf16[1024,512]{1,0:T(8,128)(2,1)}) fusion(f32[1024,512]{1,0:T(8,128)S(1)} %fusion.10, bf16[1,1024,512]{2,1,0:T(8,128)(2,1)S(1)} %copy-done.5, bf16[1,1024,512]{2,1,0:T(8,128)(2,1)S(1)} %copy-done.6, bf16[512,1024]{1,0:T(8,128)(2,1)S(1)} %bitcast.57, ...), kind=kOutput, calls=%fused_computation.5 | convolution fusion | flops 548405248 | bytes 9961472 | tf_op jit(solution)/shard_map/std,stf->sdf/dot_general | solution.py:33
  154.4 7.0 %subtract_bitcast_fusion = (f32[1,1024,512]{2,1,0:T(8,128)}, f32[1024,512]{1,0:T(8,128)}, f32[1024,512]{1,0:T(8,128)}) fusion(bf16[1024,512]{1,0:T(8,128)(2,1)S(1)} %get-tuple-element.12, bf16[1024,512]{1,0:T(8,128)(2,1)} %get-tuple-element.11, f32[1,1024,512]{2,1,0:T(8,128)S(1)} %copy-done, bf16[1024,512]{1,0:T(8,128)(2,1)} %get-tuple-element.10, ...), kind=kLoop, calls=%fused_computation.14 | loop fusion | flops 13107200 | bytes 18874368 | tf_op jit(solution)/shard_map/broadcast_in_dim | solution.py:61
  (10 shorter events, 0.0 us)
Async XLA Ops:
  37.2 38.3 %all-to-all-start = ((bf16[4,2,65536]{2,1,0:T(2,128)(2,1)}), bf16[4,2,65536]{2,1,0:T(2,128)(2,1)S(1)}, u32[]{:S(2)}, u32[]{:S(2)}) async-start(bf16[4,2,65536]{2,1,0:T(2,128)(2,1)} %reshape.40), calls=%async_computation | async-start | bytes 2097152 | tf_op jit(solution)/shard_map/all_to_all | solution.py:45
  71.9 8.7 %copy-start = (f32[1,1024,512]{2,1,0:T(8,128)S(1)}, f32[1,1024,512]{2,1,0:T(8,128)}, u32[]{:S(2)}) copy-start(f32[1,1024,512]{2,1,0:T(8,128)} %param.9) | copy-start | bytes 6291460
  75.6 64.4 %all-to-all-start.1 = ((bf16[4,2,65536]{2,1,0:T(2,128)(2,1)}), bf16[4,2,65536]{2,1,0:T(2,128)(2,1)}, u32[]{:S(2)}, u32[]{:S(2)}) async-start(bf16[4,2,65536]{2,1,0:T(2,128)(2,1)} %reshape.38), calls=%async_computation.1 | async-start | bytes 2097152 | tf_op jit(solution)/shard_map/all_to_all | solution.py:45
  80.7 73.8 %all-reduce.2.cloned.1.call-start = ((), (), s32[]{:S(2)}) async-start(), calls=%async_computation.2 | async-start | bytes 4194304 | tf_op jit(solution)/shard_map/psum | solution.py:39
  84.0 0.9 copy-start.4
  149.0 1.9 %copy-start.2 = (bf16[1,4,128,1024]{3,2,1,0:T(8,128)(2,1)S(1)}, bf16[1,4,128,1024]{3,2,1,0:T(8,128)(2,1)}, u32[]{:S(2)}) copy-start(bf16[1,4,128,1024]{3,2,1,0:T(8,128)(2,1)} %copy.19) | copy-start | bytes 3145732
  149.0 2.0 %copy-start.3 = (bf16[1,512,512]{2,1,0:T(8,128)(2,1)S(1)}, bf16[1,512,512]{2,1,0:T(8,128)(2,1)}, u32[]{:S(2)}) copy-start(bf16[1,512,512]{2,1,0:T(8,128)(2,1)} %all_gather.7) | copy-start | bytes 1572868
  149.0 2.0 %copy-start.5 = (bf16[1,1024,512]{2,1,0:T(8,128)(2,1)S(1)}, bf16[1,1024,512]{2,1,0:T(8,128)(2,1)}, u32[]{:S(2)}) copy-start(bf16[1,1024,512]{2,1,0:T(8,128)(2,1)} %param.11) | copy-start | bytes 3145732
  149.0 2.2 %copy-start.6 = (bf16[1,1024,512]{2,1,0:T(8,128)(2,1)S(1)}, bf16[1,1024,512]{2,1,0:T(8,128)(2,1)}, u32[]{:S(2)}) copy-start(bf16[1,1024,512]{2,1,0:T(8,128)(2,1)} %param.10) | copy-start | bytes 3145732
  154.4 7.0 %copy-start.1 = (bf16[1024,512]{1,0:T(8,128)(2,1)}, bf16[1024,512]{1,0:T(8,128)(2,1)S(1)}, u32[]{:S(2)}) copy-start(bf16[1024,512]{1,0:T(8,128)(2,1)S(1)} %get-tuple-element.12) | copy-start | bytes 3145732
Sparse Core Ops, SparseCore 0:
  85.3 62.8 all-reduce.1
where the time goes:
time: 169 us; the launch traced here: 168 us
  other arithmetic  56.1 us (33%)
  blocking collectives  48.4 us (29%)
  local copies, waits for them, and re-layouts  33 us (20%)
  between operations  14.1 us (8%)
  starting transfers between devices  11.4 us (7%)
  matrix products  5.23 us (3%)
    all_gather x2, blocking collectives, body(): lax.all_gather(cotangents[which:which + 1], 'fsdp', axis=1, tiled=True)  48.4 us
    unnamed x2, other arithmetic  45.8 us
    unnamed x23, local copies, waits for them, and re-layouts  26.5 us
    all_to_all x2, starting transfers between devices, body(): lax.all_to_all(inputs[which:which + 1], 'fsdp', split_axis=2, concat_axis...  11.4 us
    broadcast_in_dim x1, other arithmetic, body(): weight[None]  6.98 us
    dot_general x2, matrix products, fold_columns(): jnp.einsum('std,stf->sdf', columns, piece, preferred_element_type=jnp.flo...  5.23 us
    all_to_all x2, local copies, waits for them, and re-layouts, body(): lax.all_to_all(inputs[which:which + 1], 'fsdp', split_axis=2, concat_axis...  3.75 us
    sub x1, other arithmetic, body(): drift = anchor - weights[0]  3.39 us
  transfers between devices with their start and end apart: 3, of which 0 were waited for; matrix products, arithmetic and copies ran while one was open for 33% of the time, Pallas kernels for 0%

commit v1 on v0

v1 whole, which is shorter than its diff:
```python
import functools

import jax
import jax.numpy as jnp
from jax import lax
from jax.experimental import pallas as pl
from jax.experimental.pallas import tpu as pltpu
from jax.sharding import PartitionSpec as P

MESH = pl.DeviceIdType.MESH
F32 = jnp.float32
BF16 = jnp.bfloat16

BETA_FIRST = 0.9
BETA_SECOND = 0.95
INNER_RATE = 0.01
WEIGHT_DECAY = 0.1
EPSILON = 1e-08
OUTER_RATE = 0.7
MOMENTUM_KEEP = 0.9
MERGE_WEIGHT = 0.5


def greet(n, workers):
    barrier = pltpu.get_barrier_semaphore()
    me, worker = lax.axis_index("fsdp"), lax.axis_index("replica")
    for step in range(1, n):
        pl.semaphore_signal(
            barrier, inc=1, device_id=(worker, lax.rem(me + step, n)), device_id_type=MESH
        )
    for step in range(1, workers):
        pl.semaphore_signal(
            barrier, inc=1, device_id=(lax.rem(worker + step, workers), me), device_id_type=MESH
        )
    pl.semaphore_wait(barrier, n - 1 + workers - 1)


def exchange_kernel(n, workers, *refs):
    if workers > 1:
        (x_ref, y_ref, w_ref, a_ref, xg_ref, yg_ref, p_ref, w_vmem, a_vmem, slots, mean,
         x_send, x_recv, y_send, y_recv, own_sem, load_sem, d_send, d_recv, p_send, p_recv) = refs
    else:
        x_ref, y_ref, xg_ref, yg_ref, x_send, x_recv, y_send, y_recv, own_sem = refs
    me, worker = lax.axis_index("fsdp"), lax.axis_index("replica")
    steps, tok, din = x_ref.shape
    rows = din // n

    if workers > 1:
        load_w = pltpu.make_async_copy(w_ref, w_vmem, load_sem.at[0])
        load_a = pltpu.make_async_copy(a_ref, a_vmem, load_sem.at[1])
        load_w.start()
        load_a.start()
    greet(n, workers)

    token_rows = pl.ds(pl.multiple_of(me * tok, tok), tok)
    order = sorted(range(1, n), key=lambda d: (abs(2 * d - n), d))
    sends = []
    for s in range(steps):
        for d in order:
            peer = lax.rem(me + d, n)
            sends.append(pltpu.make_async_remote_copy(
                src_ref=y_ref.at[s], dst_ref=yg_ref.at[s, token_rows],
                send_sem=y_send.at[s, d - 1], recv_sem=y_recv.at[s, d - 1],
                device_id=(worker, peer), device_id_type=MESH))
            sends.append(pltpu.make_async_remote_copy(
                src_ref=x_ref.at[s, :, pl.ds(pl.multiple_of(peer * rows, rows), rows)],
                dst_ref=xg_ref.at[s, token_rows],
                send_sem=x_send.at[s, d - 1], recv_sem=x_recv.at[s, d - 1],
                device_id=(worker, peer), device_id_type=MESH))
    for copy in sends:
        copy.start()
    own_x = pltpu.make_async_copy(
        x_ref.at[:, :, pl.ds(pl.multiple_of(me * rows, rows), rows)],
        xg_ref.at[:, token_rows], own_sem.at[0])
    own_y = pltpu.make_async_copy(y_ref, yg_ref.at[:, token_rows], own_sem.at[1])
    own_x.start()
    own_y.start()

    if workers > 1:
        part = rows // workers
        mine = pl.ds(pl.multiple_of(worker * part, part), part)
        load_w.wait()
        load_a.wait()
        a_vmem[...] = a_vmem[...] - w_vmem[...]
        drifts, means = [], []
        for d in range(1, workers):
            peer = lax.rem(worker + d, workers)
            drifts.append(pltpu.make_async_remote_copy(
                src_ref=a_vmem.at[pl.ds(pl.multiple_of(peer * part, part), part)],
                dst_ref=slots.at[d - 1],
                send_sem=d_send.at[d - 1], recv_sem=d_recv.at[d - 1],
                device_id=(peer, me), device_id_type=MESH))
        for copy in drifts:
            copy.start()
        for copy in drifts:
            copy.wait_recv()
        summed = a_vmem[mine]
        for d in range(1, workers):
            summed = summed + slots[d - 1]
        mean[...] = summed / workers
        for d in range(1, workers):
            peer = lax.rem(worker + d, workers)
            means.append(pltpu.make_async_remote_copy(
                src_ref=mean, dst_ref=p_ref.at[mine],
                send_sem=p_send.at[d - 1], recv_sem=p_recv.at[d - 1],
                device_id=(peer, me), device_id_type=MESH))
        for copy in means:
            copy.start()
        own_p = pltpu.make_async_copy(mean, p_ref.at[mine], own_sem.at[2])
        own_p.start()
        for copy in drifts:
            copy.wait_send()
        for copy in means:
            copy.wait()
        own_p.wait()
    own_x.wait()
    own_y.wait()
    for copy in sends:
        copy.wait()


def exchange(n, workers, inputs, cotangents, weight, anchor):
    steps, tok, din = inputs.shape
    width = cotangents.shape[2]
    rows = din // n
    outs = [
        jax.ShapeDtypeStruct((steps, n * tok, rows), inputs.dtype),
        jax.ShapeDtypeStruct((steps, n * tok, width), cotangents.dtype),
    ]
    operands = [inputs, cotangents]
    near = pltpu.SemaphoreType.DMA((steps, n - 1))
    scratch = [near] * 4 + [pltpu.SemaphoreType.DMA((3,))]
    if workers > 1:
        part = rows // workers
        far = pltpu.SemaphoreType.DMA((workers - 1,))
        outs.append(jax.ShapeDtypeStruct((rows, width), F32))
        operands += [weight, anchor]
        scratch = [
            pltpu.VMEM((rows, width), F32),
            pltpu.VMEM((rows, width), F32),
            pltpu.VMEM((workers - 1, part, width), F32),
            pltpu.VMEM((part, width), F32),
        ] + scratch + [pltpu.SemaphoreType.DMA((2,))] + [far] * 4
    return pl.pallas_call(
        functools.partial(exchange_kernel, n, workers),
        out_shape=outs,
        in_specs=[pl.BlockSpec(memory_space=pl.ANY)] * len(operands),
        out_specs=[pl.BlockSpec(memory_space=pl.ANY)] * len(outs),
        scratch_shapes=scratch,
        compiler_params=pltpu.CompilerParams(
            collective_id=0, has_side_effects=True, vmem_limit_bytes=16 * 2**20
        ),
        name="exchange",
    )(*operands)


def update_kernel(x_ref, y_ref, w_ref, m_ref, v_ref, a_ref, o_ref, p_ref,
                  w_out, m_out, v_out, a_out, o_out):
    anchor, pseudo = a_ref[...], p_ref[...]
    momentum = MOMENTUM_KEEP * o_ref[...] + pseudo
    anchor_new = anchor - OUTER_RATE * (pseudo + MOMENTUM_KEEP * momentum)
    o_out[...] = momentum
    a_out[...] = anchor_new
    weight, first, second = w_ref[0], m_ref[0], v_ref[0]
    for s in range(x_ref.shape[0]):
        gradient = lax.dot_general(
            x_ref[s], y_ref[s], (((0,), (0,)), ((), ())), preferred_element_type=F32
        )
        first = (BETA_FIRST * first.astype(F32) + (1.0 - BETA_FIRST) * gradient).astype(BF16)
        second = (
            BETA_SECOND * second.astype(F32) + (1.0 - BETA_SECOND) * gradient * gradient
        ).astype(BF16)
        weight = weight - INNER_RATE * (
            first.astype(F32) / (jnp.sqrt(second.astype(F32)) + EPSILON) + WEIGHT_DECAY * weight
        )
        if s == 0:
            weight = MERGE_WEIGHT * weight + (1.0 - MERGE_WEIGHT) * anchor_new
    w_out[0] = weight
    m_out[0] = first
    v_out[0] = second


def update(gathered, upstream, weights, first, second, anchor, outer, pseudo):
    steps, tokens, rows = gathered.shape
    width = upstream.shape[2]
    block = min(128, rows)
    state = pl.BlockSpec((1, block, width), lambda i: (0, i, 0))
    plain = pl.BlockSpec((block, width), lambda i: (i, 0))
    shape = lambda ref: jax.ShapeDtypeStruct(ref.shape, ref.dtype)
    return pl.pallas_call(
        update_kernel,
        grid=(rows // block,),
        in_specs=[
            pl.BlockSpec((steps, tokens, block), lambda i: (0, 0, i)),
            pl.BlockSpec((steps, tokens, width), lambda i: (0, 0, 0)),
            state, state, state, plain, plain, plain,
        ],
        out_specs=[state, state, state, plain, plain],
        out_shape=[shape(weights), shape(first), shape(second), shape(anchor), shape(outer)],
        compiler_params=pltpu.CompilerParams(vmem_limit_bytes=40 * 2**20),
        name="update",
    )(gathered, upstream, weights, first, second, anchor, outer, pseudo)


def solution(mesh):
    n, workers = mesh.shape["fsdp"], mesh.shape["replica"]

    def body(inputs, cotangents, weights, first, second, anchor, outer):
        rows = anchor.shape[0]
        if rows % (16 * workers) == 0:
            gathered, upstream, pseudo = exchange(
                n, workers, inputs, cotangents, weights[0], anchor
            )
        else:
            gathered, upstream = exchange(n, 1, inputs, cotangents, None, None)
            pseudo = lax.psum(anchor - weights[0], "replica") / workers
        return tuple(update(gathered, upstream, weights, first, second, anchor, outer, pseudo))

    in_specs = (
        P(None, ("replica", "fsdp"), None),
        P(None, ("replica", "fsdp"), None),
        P("replica", "fsdp", None),
        P("replica", "fsdp", None),
        P("replica", "fsdp", None),
        P("fsdp", None),
        P("fsdp", None),
    )
    out_specs = (
        P("replica", "fsdp", None),
        P("replica", "fsdp", None),
        P("replica", "fsdp", None),
        P("fsdp", None),
        P("fsdp", None),
    )
    return jax.shard_map(body, mesh=mesh, in_specs=in_specs, out_specs=out_specs, check_vma=False)
```

time: 169 us -> 90.3 us (0.53)
  the two profiles are of different devices: /device:TPU:0 before, /device:TPU:8 now
where the time goes in v1:
time: 90.3 us; the launch traced here: 90 us
  Pallas kernels  81.1 us (90%)
  local copies, waits for them, and re-layouts  8.17 us (9%)
    pallas_call x1, Pallas kernels, exchange(): pl.pallas_call(functools.partial(exchange_kernel, n, workers), out_shape=...  73.4 us
    unnamed x18, local copies, waits for them, and re-layouts  8.17 us
    pallas_call x1, Pallas kernels, update(): pl.pallas_call(update_kernel, grid=(rows // block,), in_specs=[pl.BlockSp...  7.74 us

profile of v1, /device:TPU:8, one launch (start us, length us, event | category | flops | bytes accessed | tf_op | source)
XLA Modules:
  0.0 90.0 jit_solution(1563275161664494793)
XLA Ops:
  0.6 0.0 copy-start
  0.6 1.6 %copy-done = f32[1,1024,512]{2,1,0:T(8,128)S(1)} copy-done((f32[1,1024,512]{2,1,0:T(8,128)S(1)}, f32[1,1024,512]{2,1,0:T(8,128)}, u32[]{:S(2)}) %copy-start) | copy-done | bytes 2097176
  2.2 0.0 copy-start.2
  2.2 1.6 %copy-done.2 = f32[1024,512]{1,0:T(8,128)S(1)} copy-done((f32[1024,512]{1,0:T(8,128)S(1)}, f32[1024,512]{1,0:T(8,128)}, u32[]{:S(2)}) %copy-start.2) | copy-done | bytes 2097176
  3.8 0.0 copy-start.4
  3.8 1.6 %copy-done.4 = bf16[2,128,4096]{2,1,0:T(8,128)(2,1)S(1)} copy-done((bf16[2,128,4096]{2,1,0:T(8,128)(2,1)S(1)}, bf16[2,128,4096]{2,1,0:T(8,128)(2,1)}, u32[]{:S(2)}) %copy-start.4) | copy-done | bytes 2097176
  5.4 0.0 copy-start.8
  5.4 0.9 %copy-done.8 = bf16[2,128,512]{2,1,0:T(8,128)(2,1)S(1)} copy-done((bf16[2,128,512]{2,1,0:T(8,128)(2,1)S(1)}, bf16[2,128,512]{2,1,0:T(8,128)(2,1)}, u32[]{:S(2)}) %copy-start.8) | copy-done | bytes 262168
  6.4 0.0 copy-start.1
  6.4 0.0 copy-start.3
  6.4 0.0 copy-start.5
  6.4 73.4 %exchange.1 = (bf16[2,512,1024]{2,1,0:T(8,128)(2,1)S(1)}, bf16[2,512,512]{2,1,0:T(8,128)(2,1)S(1)}, f32[1024,512]{1,0:T(8,128)S(1)}) custom-call(bf16[2,128,4096]{2,1,0:T(8,128)(2,1)S(1)} %copy-done.4, bf16[2,128,512]{2,1,0:T(8,128)(2,1)S(1)} %copy-done.8, f32[1024,512]{1,0:T(8,128)S(1)} %bitcast.1, f32[1024,512]{1,0:T(8,128)S(1)} %copy-done.2), custom_call_target="tpu_custom_call" | custom-call | tf_op jit(solution)/shard_map/exchange/pallas_call | solution.py:144
  79.7 0.0 copy-done.1
  79.7 0.0 copy-done.3
  79.8 0.0 copy-done.5
  79.8 0.0 copy-start.6
  79.8 1.2 %copy-done.6 = bf16[1,1024,512]{2,1,0:T(8,128)(2,1)S(1)} copy-done((bf16[1,1024,512]{2,1,0:T(8,128)(2,1)S(1)}, bf16[1,1024,512]{2,1,0:T(8,128)(2,1)}, u32[]{:S(2)}) %copy-start.6) | copy-done | bytes 1048600
  81.0 0.0 copy-start.7
  81.0 1.2 %copy-done.7 = bf16[1,1024,512]{2,1,0:T(8,128)(2,1)S(1)} copy-done((bf16[1,1024,512]{2,1,0:T(8,128)(2,1)S(1)}, bf16[1,1024,512]{2,1,0:T(8,128)(2,1)}, u32[]{:S(2)}) %copy-start.7) | copy-done | bytes 1048600
  82.2 7.7 %update.1 = (f32[1,1024,512]{2,1,0:T(8,128)}, bf16[1,1024,512]{2,1,0:T(8,128)(2,1)}, bf16[1,1024,512]{2,1,0:T(8,128)(2,1)}, f32[1024,512]{1,0:T(8,128)}, f32[1024,512]{1,0:T(8,128)}) custom-call(bf16[2,512,1024]{2,1,0:T(8,128)(2,1)S(1)} %get-tuple-element.8.x_ref, bf16[2,512,512]{2,1,0:T(8,128)(2,1)S(1)} %get-tuple-element.9.y_ref, ...), custom_call_target="tpu_custom_call" | custom-call | tf_op jit(solution)/shard_map/update/pallas_call | solution.py:190
Async XLA Ops:
  0.6 1.6 %copy-start = (f32[1,1024,512]{2,1,0:T(8,128)S(1)}, f32[1,1024,512]{2,1,0:T(8,128)}, u32[]{:S(2)}) copy-start(f32[1,1024,512]{2,1,0:T(8,128)} %w_ref.1) | copy-start | bytes 6291460
  2.2 1.6 %copy-start.2 = (f32[1024,512]{1,0:T(8,128)S(1)}, f32[1024,512]{1,0:T(8,128)}, u32[]{:S(2)}) copy-start(f32[1024,512]{1,0:T(8,128)} %a_ref.1) | copy-start | bytes 6291460
  3.8 1.6 %copy-start.4 = (bf16[2,128,4096]{2,1,0:T(8,128)(2,1)S(1)}, bf16[2,128,4096]{2,1,0:T(8,128)(2,1)}, u32[]{:S(2)}) copy-start(bf16[2,128,4096]{2,1,0:T(8,128)(2,1)} %refs_0_.1) | copy-start | bytes 6291460
  5.4 0.9 %copy-start.8 = (bf16[2,128,512]{2,1,0:T(8,128)(2,1)S(1)}, bf16[2,128,512]{2,1,0:T(8,128)(2,1)}, u32[]{:S(2)}) copy-start(bf16[2,128,512]{2,1,0:T(8,128)(2,1)} %refs_1_.1) | copy-start | bytes 786436
  6.4 73.4 %copy-start.1 = (f32[1,1024,512]{2,1,0:T(8,128)S(1)}, f32[1,1024,512]{2,1,0:T(8,128)}, u32[]{:S(2)}) copy-start(f32[1,1024,512]{2,1,0:T(8,128)} %w_ref.1) | copy-start | bytes 6291460
  6.4 73.4 %copy-start.3 = (f32[1024,512]{1,0:T(8,128)S(1)}, f32[1024,512]{1,0:T(8,128)}, u32[]{:S(2)}) copy-start(f32[1024,512]{1,0:T(8,128)} %a_ref.1) | copy-start | bytes 6291460
  6.4 73.4 %copy-start.5 = (f32[1024,512]{1,0:T(8,128)S(1)}, f32[1024,512]{1,0:T(8,128)}, u32[]{:S(2)}) copy-start(f32[1024,512]{1,0:T(8,128)} %o_ref.1) | copy-start | bytes 6291460
  79.8 1.2 %copy-start.6 = (bf16[1,1024,512]{2,1,0:T(8,128)(2,1)S(1)}, bf16[1,1024,512]{2,1,0:T(8,128)(2,1)}, u32[]{:S(2)}) copy-start(bf16[1,1024,512]{2,1,0:T(8,128)(2,1)} %m_ref.1) | copy-start | bytes 3145732
  81.0 1.2 %copy-start.7 = (bf16[1,1024,512]{2,1,0:T(8,128)(2,1)S(1)}, bf16[1,1024,512]{2,1,0:T(8,128)(2,1)}, u32[]{:S(2)}) copy-start(bf16[1,1024,512]{2,1,0:T(8,128)(2,1)} %v_ref.1) | copy-start | bytes 3145732

commit v2 on v1

--- a/solution.py
+++ b/solution.py
@@ -19,6 +19,8 @@
 OUTER_RATE = 0.7
 MOMENTUM_KEEP = 0.9
 MERGE_WEIGHT = 0.5
+EXCHANGE_VMEM = 60 * 2**20
+UPDATE_VMEM = 60 * 2**20
 
 
 def greet(n, workers):
@@ -33,6 +35,17 @@
             barrier, inc=1, device_id=(lax.rem(worker + step, workers), me), device_id_type=MESH
         )
     pl.semaphore_wait(barrier, n - 1 + workers - 1)
+
+
+def partner(me, k, n):
+    if n & (n - 1):
+        return lax.rem(me + k, n)
+    peer, bit = me, 1
+    while bit < n:
+        if k & bit:
+            peer = peer + (1 - 2 * (me // bit % 2)) * bit
+        bit *= 2
+    return peer
 
 
 def exchange_kernel(n, workers, *refs):
@@ -53,19 +66,45 @@
     greet(n, workers)
 
     token_rows = pl.ds(pl.multiple_of(me * tok, tok), tok)
-    order = sorted(range(1, n), key=lambda d: (abs(2 * d - n), d))
+    right, left = lax.rem(me + 1, n), lax.rem(me + n - 1, n)
+
+    def hop(h, way):
+        to_right = way == 0
+        origin = me - (h - 1) if to_right else me + (h - 1)
+        sends_it = jnp.logical_and(origin >= 0, me < n - 1) if to_right else jnp.logical_and(
+            origin < n, me > 0)
+        comes = me >= h if to_right else me + h < n
+        held = pl.ds(pl.multiple_of(lax.rem(origin + n, n) * tok, tok), tok)
+        copy = pltpu.make_async_remote_copy(
+            src_ref=y_ref if h == 1 else yg_ref.at[:, held], dst_ref=yg_ref.at[:, held],
+            send_sem=y_send.at[way, h - 1], recv_sem=y_recv.at[way, h - 1],
+            device_id=(worker, right if to_right else left), device_id_type=MESH)
+        return copy, sends_it, comes
+
+    def hop_start(h):
+        for way in range(2):
+            copy, sends_it, _ = hop(h, way)
+            pl.when(sends_it)(copy.start)
+
+    def hop_arrived(h):
+        for way in range(2):
+            copy, _, comes = hop(h, way)
+            pl.when(comes)(copy.wait_recv)
+
+    def pass_on():
+        for h in range(3, n):
+            hop_arrived(h - 1)
+            hop_start(h)
+
+    hop_start(1)
     sends = []
-    for s in range(steps):
-        for d in order:
-            peer = lax.rem(me + d, n)
-            sends.append(pltpu.make_async_remote_copy(
-                src_ref=y_ref.at[s], dst_ref=yg_ref.at[s, token_rows],
-                send_sem=y_send.at[s, d - 1], recv_sem=y_recv.at[s, d - 1],
-                device_id=(worker, peer), device_id_type=MESH))
+    for k in range(n - 1, 0, -1):
+        for s in range(steps):
+            peer = partner(me, k, n)
             sends.append(pltpu.make_async_remote_copy(
                 src_ref=x_ref.at[s, :, pl.ds(pl.multiple_of(peer * rows, rows), rows)],
                 dst_ref=xg_ref.at[s, token_rows],
-                send_sem=x_send.at[s, d - 1], recv_sem=x_recv.at[s, d - 1],
+                send_sem=x_send.at[s, k - 1], recv_sem=x_recv.at[s, k - 1],
                 device_id=(worker, peer), device_id_type=MESH))
     for copy in sends:
         copy.start()
@@ -92,6 +131,9 @@
                 device_id=(peer, me), device_id_type=MESH))
         for copy in drifts:
             copy.start()
+        if n > 2:
+            hop_arrived(1)
+            hop_start(2)
         for copy in drifts:
             copy.wait_recv()
         summed = a_vmem[mine]
@@ -108,13 +150,24 @@
             copy.start()
         own_p = pltpu.make_async_copy(mean, p_ref.at[mine], own_sem.at[2])
         own_p.start()
+        pass_on()
         for copy in drifts:
             copy.wait_send()
         for copy in means:
             copy.wait()
         own_p.wait()
+    else:
+        if n > 2:
+            hop_arrived(1)
+            hop_start(2)
+        pass_on()
     own_x.wait()
     own_y.wait()
+    hop_arrived(n - 1)
+    for h in range(1, n):
+        for way in range(2):
+            copy, sends_it, _ = hop(h, way)
+            pl.when(sends_it)(copy.wait_send)
     for copy in sends:
         copy.wait()
 
@@ -129,7 +182,8 @@
     ]
     operands = [inputs, cotangents]
     near = pltpu.SemaphoreType.DMA((steps, n - 1))
-    scratch = [near] * 4 + [pltpu.SemaphoreType.DMA((3,))]
+    chain = pltpu.SemaphoreType.DMA((2, n - 1))
+    scratch = [near] * 2 + [chain] * 2 + [pltpu.SemaphoreType.DMA((3,))]
     if workers > 1:
         part = rows // workers
         far = pltpu.SemaphoreType.DMA((workers - 1,))
@@ -148,7 +202,7 @@
         out_specs=[pl.BlockSpec(memory_space=pl.ANY)] * len(outs),
         scratch_shapes=scratch,
         compiler_params=pltpu.CompilerParams(
-            collective_id=0, has_side_effects=True, vmem_limit_bytes=16 * 2**20
+            collective_id=0, has_side_effects=True, vmem_limit_bytes=EXCHANGE_VMEM
         ),
         name="exchange",
     )(*operands)
@@ -183,7 +237,7 @@
 def update(gathered, upstream, weights, first, second, anchor, outer, pseudo):
     steps, tokens, rows = gathered.shape
     width = upstream.shape[2]
-    block = min(128, rows)
+    block = min(256, rows)
     state = pl.BlockSpec((1, block, width), lambda i: (0, i, 0))
     plain = pl.BlockSpec((block, width), lambda i: (i, 0))
     shape = lambda ref: jax.ShapeDtypeStruct(ref.shape, ref.dtype)
@@ -197,7 +251,7 @@
         ],
         out_specs=[state, state, state, plain, plain],
         out_shape=[shape(weights), shape(first), shape(second), shape(anchor), shape(outer)],
-        compiler_params=pltpu.CompilerParams(vmem_limit_bytes=40 * 2**20),
+        compiler_params=pltpu.CompilerParams(vmem_limit_bytes=UPDATE_VMEM),
         name="update",
     )(gathered, upstream, weights, first, second, anchor, outer, pseudo)
 

time: 90.3 us -> 83.5 us (0.925)
  the two profiles are of different devices: /device:TPU:8 before, /device:TPU:0 now
where the time goes in v2:
time: 83.5 us; the launch traced here: 83.4 us
  Pallas kernels  82.7 us (99%)
    pallas_call x1, Pallas kernels, exchange(): pl.pallas_call(functools.partial(exchange_kernel, n, workers), out_shape=...  71.6 us
    pallas_call x1, Pallas kernels, update(): pl.pallas_call(update_kernel, grid=(rows // block,), in_specs=[pl.BlockSp...  11.1 us

profile of v2, /device:TPU:0, one launch (start us, length us, event | category | flops | bytes accessed | tf_op | source)
XLA Modules:
  0.0 83.4 jit_solution(5645444731893531027)
XLA Ops:
  0.6 71.6 %exchange.1 = (bf16[2,512,1024]{2,1,0:T(8,128)(2,1)}, bf16[2,512,512]{2,1,0:T(8,128)(2,1)}, f32[1024,512]{1,0:T(8,128)}) custom-call(bf16[2,128,4096]{2,1,0:T(8,128)(2,1)} %refs_0_.1, bf16[2,128,512]{2,1,0:T(8,128)(2,1)} %refs_1_.1, f32[1024,512]{1,0:T(8,128)} %bitcast.1, f32[1024,512]{1,0:T(8,128)} %a_ref.1), custom_call_target="tpu_custom_call" | custom-call | tf_op jit(solution)/shard_map/exchange/pallas_call | solution.py:198
  72.2 11.1 %update.1 = (f32[1,1024,512]{2,1,0:T(8,128)}, bf16[1,1024,512]{2,1,0:T(8,128)(2,1)}, bf16[1,1024,512]{2,1,0:T(8,128)(2,1)}, f32[1024,512]{1,0:T(8,128)}, f32[1024,512]{1,0:T(8,128)}) custom-call(bf16[2,512,1024]{2,1,0:T(8,128)(2,1)} %get-tuple-element.8.x_ref, bf16[2,512,512]{2,1,0:T(8,128)(2,1)} %get-tuple-element.9.y_ref, f32[1,1024,512]{2,1,0:T(8,128)} %w_ref.1, ...), custom_call_target="tpu_custom_call" | custom-call | tf_op jit(solution)/shard_map/update/pallas_call | solution.py:244

commit v3 on v2

--- a/solution.py
+++ b/solution.py
@@ -19,8 +19,9 @@
 OUTER_RATE = 0.7
 MOMENTUM_KEEP = 0.9
 MERGE_WEIGHT = 0.5
-EXCHANGE_VMEM = 60 * 2**20
+EXCHANGE_VMEM = 52 * 2**20
 UPDATE_VMEM = 60 * 2**20
+FINISH_VMEM = 28 * 2**20
 
 
 def greet(n, workers):
@@ -50,8 +51,11 @@
 
 def exchange_kernel(n, workers, *refs):
     if workers > 1:
-        (x_ref, y_ref, w_ref, a_ref, xg_ref, yg_ref, p_ref, w_vmem, a_vmem, slots, mean,
-         x_send, x_recv, y_send, y_recv, own_sem, load_sem, d_send, d_recv, p_send, p_recv) = refs
+        x_ref, y_ref, *state = refs[:7]
+        xg_ref, yg_ref, *held = refs[7:14]
+        weight, anchor, first, second, momentum = held
+        (drift, slots, pseudo, x_send, x_recv, y_send, y_recv, own_sem, load_sem, d_send, d_recv,
+         p_send, p_recv) = refs[14:]
     else:
         x_ref, y_ref, xg_ref, yg_ref, x_send, x_recv, y_send, y_recv, own_sem = refs
     me, worker = lax.axis_index("fsdp"), lax.axis_index("replica")
@@ -59,10 +63,12 @@
     rows = din // n
 
     if workers > 1:
-        load_w = pltpu.make_async_copy(w_ref, w_vmem, load_sem.at[0])
-        load_a = pltpu.make_async_copy(a_ref, a_vmem, load_sem.at[1])
-        load_w.start()
-        load_a.start()
+        loads = [
+            pltpu.make_async_copy(src, dst, load_sem.at[i])
+            for i, (src, dst) in enumerate(zip(state, held))
+        ]
+        for copy in loads:
+            copy.start()
     greet(n, workers)
 
     token_rows = pl.ds(pl.multiple_of(me * tok, tok), tok)
@@ -98,15 +104,15 @@
 
     hop_start(1)
     sends = []
-    for k in range(n - 1, 0, -1):
-        for s in range(steps):
+    for s in range(steps):
+        for k in range(n - 1, 0, -1):
             peer = partner(me, k, n)
             sends.append(pltpu.make_async_remote_copy(
                 src_ref=x_ref.at[s, :, pl.ds(pl.multiple_of(peer * rows, rows), rows)],
                 dst_ref=xg_ref.at[s, token_rows],
                 send_sem=x_send.at[s, k - 1], recv_sem=x_recv.at[s, k - 1],
                 device_id=(worker, peer), device_id_type=MESH))
-    for copy in sends:
+    for copy in (sends[:n - 1] if workers > 1 else sends):
         copy.start()
     own_x = pltpu.make_async_copy(
         x_ref.at[:, :, pl.ds(pl.multiple_of(me * rows, rows), rows)],
@@ -118,14 +124,14 @@
     if workers > 1:
         part = rows // workers
         mine = pl.ds(pl.multiple_of(worker * part, part), part)
-        load_w.wait()
-        load_a.wait()
-        a_vmem[...] = a_vmem[...] - w_vmem[...]
+        loads[0].wait()
+        loads[1].wait()
+        drift[...] = anchor[...] - weight[...]
         drifts, means = [], []
         for d in range(1, workers):
             peer = lax.rem(worker + d, workers)
             drifts.append(pltpu.make_async_remote_copy(
-                src_ref=a_vmem.at[pl.ds(pl.multiple_of(peer * part, part), part)],
+                src_ref=drift.at[pl.ds(pl.multiple_of(peer * part, part), part)],
                 dst_ref=slots.at[d - 1],
                 send_sem=d_send.at[d - 1], recv_sem=d_recv.at[d - 1],
                 device_id=(peer, me), device_id_type=MESH))
@@ -134,45 +140,85 @@
         if n > 2:
             hop_arrived(1)
             hop_start(2)
+        sends[0].wait_send()
+        sends[n - 1].start()
         for copy in drifts:
             copy.wait_recv()
-        summed = a_vmem[mine]
+        summed = drift[mine]
         for d in range(1, workers):
             summed = summed + slots[d - 1]
-        mean[...] = summed / workers
+        pseudo[mine] = summed / workers
         for d in range(1, workers):
             peer = lax.rem(worker + d, workers)
             means.append(pltpu.make_async_remote_copy(
-                src_ref=mean, dst_ref=p_ref.at[mine],
+                src_ref=pseudo.at[mine], dst_ref=pseudo.at[mine],
                 send_sem=p_send.at[d - 1], recv_sem=p_recv.at[d - 1],
                 device_id=(peer, me), device_id_type=MESH))
         for copy in means:
             copy.start()
-        own_p = pltpu.make_async_copy(mean, p_ref.at[mine], own_sem.at[2])
-        own_p.start()
+        for copy in sends[1:n - 1]:
+            copy.wait_send()
+        for copy in sends[n:]:
+            copy.start()
         pass_on()
-        for copy in drifts:
+        for copy in loads[2:]:
+            copy.wait()
+        own_x.wait()
+        own_y.wait()
+        hop_arrived(n - 1)
+        for copy in sends[:n - 1]:
+            copy.wait_recv()
+        for copy in means:
+            copy.wait_recv()
+        block = min(128, rows)
+
+        @pl.loop(0, rows // block)
+        def _(i):
+            at = pl.ds(pl.multiple_of(i * block, block), block)
+            weight[at], first[at], second[at] = inner(
+                xg_ref[0, :, at], yg_ref[0], weight[at], first[at], second[at])
+            mean = pseudo[at]
+            kept = MOMENTUM_KEEP * momentum[at] + mean
+            momentum[at] = kept
+            merged = anchor[at] - OUTER_RATE * (mean + MOMENTUM_KEEP * kept)
+            anchor[at] = merged
+            weight[at] = MERGE_WEIGHT * weight[at] + (1.0 - MERGE_WEIGHT) * merged
+
+        for copy in drifts + means:
             copy.wait_send()
-        for copy in means:
+        for copy in sends[n - 1:]:
             copy.wait()
-        own_p.wait()
     else:
         if n > 2:
             hop_arrived(1)
             hop_start(2)
         pass_on()
-    own_x.wait()
-    own_y.wait()
-    hop_arrived(n - 1)
+        own_x.wait()
+        own_y.wait()
+        hop_arrived(n - 1)
+        for copy in sends:
+            copy.wait()
     for h in range(1, n):
         for way in range(2):
             copy, sends_it, _ = hop(h, way)
             pl.when(sends_it)(copy.wait_send)
-    for copy in sends:
-        copy.wait()
-
-
-def exchange(n, workers, inputs, cotangents, weight, anchor):
+
+
+def inner(features, upstream, weight, first, second):
+    gradient = lax.dot_general(
+        features, upstream, (((0,), (0,)), ((), ())), preferred_element_type=F32
+    )
+    first = (BETA_FIRST * first.astype(F32) + (1.0 - BETA_FIRST) * gradient).astype(BF16)
+    second = (
+        BETA_SECOND * second.astype(F32) + (1.0 - BETA_SECOND) * gradient * gradient
+    ).astype(BF16)
+    weight = weight - INNER_RATE * (
+        first.astype(F32) / (jnp.sqrt(second.astype(F32)) + EPSILON) + WEIGHT_DECAY * weight
+    )
+    return weight, first, second
+
+
+def exchange(n, workers, inputs, cotangents, *state):
     steps, tok, din = inputs.shape
     width = cotangents.shape[2]
     rows = din // n
@@ -187,19 +233,18 @@
     if workers > 1:
         part = rows // workers
         far = pltpu.SemaphoreType.DMA((workers - 1,))
-        outs.append(jax.ShapeDtypeStruct((rows, width), F32))
-        operands += [weight, anchor]
+        outs = [pltpu.VMEM(out.shape, out.dtype) for out in outs + list(state)]
+        operands += state
         scratch = [
             pltpu.VMEM((rows, width), F32),
+            pltpu.VMEM((workers - 1, part, width), F32),
             pltpu.VMEM((rows, width), F32),
-            pltpu.VMEM((workers - 1, part, width), F32),
-            pltpu.VMEM((part, width), F32),
-        ] + scratch + [pltpu.SemaphoreType.DMA((2,))] + [far] * 4
+        ] + scratch + [pltpu.SemaphoreType.DMA((5,))] + [far] * 4
     return pl.pallas_call(
         functools.partial(exchange_kernel, n, workers),
         out_shape=outs,
         in_specs=[pl.BlockSpec(memory_space=pl.ANY)] * len(operands),
-        out_specs=[pl.BlockSpec(memory_space=pl.ANY)] * len(outs),
+        out_specs=[pl.BlockSpec(memory_space=pltpu.VMEM if workers > 1 else pl.ANY)] * len(outs),
         scratch_shapes=scratch,
         compiler_params=pltpu.CompilerParams(
             collective_id=0, has_side_effects=True, vmem_limit_bytes=EXCHANGE_VMEM
@@ -217,16 +262,7 @@
     a_out[...] = anchor_new
     weight, first, second = w_ref[0], m_ref[0], v_ref[0]
     for s in range(x_ref.shape[0]):
-        gradient = lax.dot_general(
-            x_ref[s], y_ref[s], (((0,), (0,)), ((), ())), preferred_element_type=F32
-        )
-        first = (BETA_FIRST * first.astype(F32) + (1.0 - BETA_FIRST) * gradient).astype(BF16)
-        second = (
-            BETA_SECOND * second.astype(F32) + (1.0 - BETA_SECOND) * gradient * gradient
-        ).astype(BF16)
-        weight = weight - INNER_RATE * (
-            first.astype(F32) / (jnp.sqrt(second.astype(F32)) + EPSILON) + WEIGHT_DECAY * weight
-        )
+        weight, first, second = inner(x_ref[s], y_ref[s], weight, first, second)
         if s == 0:
             weight = MERGE_WEIGHT * weight + (1.0 - MERGE_WEIGHT) * anchor_new
     w_out[0] = weight
@@ -256,18 +292,52 @@
     )(gathered, upstream, weights, first, second, anchor, outer, pseudo)
 
 
+def finish_kernel(x_ref, y_ref, w_ref, a_ref, m_ref, v_ref, o_ref, w_out, m_out, v_out, a_out, o_out):
+    o_out[...] = o_ref[...]
+    a_out[...] = a_ref[...]
+    weight, first, second = w_ref[...], m_ref[...], v_ref[...]
+    for s in range(x_ref.shape[0]):
+        weight, first, second = inner(x_ref[s], y_ref[s], weight, first, second)
+    w_out[0] = weight
+    m_out[0] = first
+    v_out[0] = second
+
+
+def finish(gathered, upstream, weight, anchor, first, second, momentum):
+    steps, tokens, rows = gathered.shape
+    width = upstream.shape[2]
+    block = min(256, rows)
+    state = pl.BlockSpec((1, block, width), lambda i: (0, i, 0))
+    plain = pl.BlockSpec((block, width), lambda i: (i, 0))
+    shape = lambda ref: jax.ShapeDtypeStruct(ref.shape, ref.dtype)
+    lead = lambda ref: jax.ShapeDtypeStruct((1,) + ref.shape, ref.dtype)
+    later = steps - 1
+    return pl.pallas_call(
+        finish_kernel,
+        grid=(rows // block,),
+        in_specs=[
+            pl.BlockSpec((later, tokens, block), lambda i: (1, 0, i)),
+            pl.BlockSpec((later, tokens, width), lambda i: (1, 0, 0)),
+            plain, plain, plain, plain, plain,
+        ],
+        out_specs=[state, state, state, plain, plain],
+        out_shape=[lead(weight), lead(first), lead(second), shape(anchor), shape(momentum)],
+        compiler_params=pltpu.CompilerParams(vmem_limit_bytes=FINISH_VMEM),
+        name="finish",
+    )(gathered, upstream, weight, anchor, first, second, momentum)
+
+
 def solution(mesh):
     n, workers = mesh.shape["fsdp"], mesh.shape["replica"]
 
     def body(inputs, cotangents, weights, first, second, anchor, outer):
         rows = anchor.shape[0]
-        if rows % (16 * workers) == 0:
-            gathered, upstream, pseudo = exchange(
-                n, workers, inputs, cotangents, weights[0], anchor
-            )
-        else:
-            gathered, upstream = exchange(n, 1, inputs, cotangents, None, None)
-            pseudo = lax.psum(anchor - weights[0], "replica") / workers
+        if rows % (16 * workers) == 0 and inputs.shape[0] == 2:
+            return tuple(finish(*exchange(
+                n, workers, inputs, cotangents, weights[0], anchor, first[0], second[0], outer
+            )))
+        gathered, upstream = exchange(n, 1, inputs, cotangents)
+        pseudo = lax.psum(anchor - weights[0], "replica") / workers
         return tuple(update(gathered, upstream, weights, first, second, anchor, outer, pseudo))
 
     in_specs = (

time: 83.5 us -> 75.5 us (0.904)
  Pallas kernels: 82.7 us -> 74.7 us
    pallas_call x1, Pallas kernels: 11.1 us -> 4.87 us  [finish(): pl.pallas_call(finish_kernel, grid=(rows // block,), in_specs=[pl.BlockSp...]
    pallas_call x1, Pallas kernels: 71.6 us -> 69.8 us  [exchange(): pl.pallas_call(functools.partial(exchange_kernel, n, workers), out_shape=...]
where the time goes in v3:
time: 75.5 us; the launch traced here: 75.3 us
  Pallas kernels  74.7 us (99%)
    pallas_call x1, Pallas kernels, exchange(): pl.pallas_call(functools.partial(exchange_kernel, n, workers), out_shape=...  69.8 us
    pallas_call x1, Pallas kernels, finish(): pl.pallas_call(finish_kernel, grid=(rows // block,), in_specs=[pl.BlockSp...  4.87 us

profile of v3, /device:TPU:0, one launch (start us, length us, event | category | flops | bytes accessed | tf_op | source)
XLA Modules:
  0.0 75.3 jit_solution(9947811673062040508)
XLA Ops:
  0.6 69.8 %exchange.1 = (bf16[2,512,1024]{2,1,0:T(8,128)(2,1)S(1)}, bf16[2,512,512]{2,1,0:T(8,128)(2,1)S(1)}, f32[1024,512]{1,0:T(8,128)S(1)}, f32[1024,512]{1,0:T(8,128)S...) custom-call(bf16[2,128,4096]{2,1,0:T(8,128)(2,1)} %refs_0_.1, ...), custom_call_target="tpu_custom_call" | custom-call | tf_op jit(solution)/shard_map/exchange/pallas_call | solution.py:243
  70.5 4.9 %finish.1 = (f32[1,1024,512]{2,1,0:T(8,128)}, bf16[1,1024,512]{2,1,0:T(8,128)(2,1)}, bf16[1,1024,512]{2,1,0:T(8,128)(2,1)}, f32[1024,512]{1,0:T(8,128)}, f32[1024,512]{1,0:T(8,128)}) custom-call(bf16[2,512,1024]{2,1,0:T(8,128)(2,1)S(1)} %get-tuple-element.12.x_ref, bf16[2,512,512]{2,1,0:T(8,128)(2,1)S(1)} %get-tuple-element.13.y_ref, ...), custom_call_target="tpu_custom_call" | custom-call | tf_op jit(solution)/shard_map/finish/pallas_call | solution.py:315

commit v4 on v3

--- a/solution.py
+++ b/solution.py
@@ -140,8 +140,6 @@
         if n > 2:
             hop_arrived(1)
             hop_start(2)
-        sends[0].wait_send()
-        sends[n - 1].start()
         for copy in drifts:
             copy.wait_recv()
         summed = drift[mine]
@@ -156,10 +154,9 @@
                 device_id=(peer, me), device_id_type=MESH))
         for copy in means:
             copy.start()
-        for copy in sends[1:n - 1]:
+        for copy, later in zip(sends[:n - 1], sends[n - 1:]):
             copy.wait_send()
-        for copy in sends[n:]:
-            copy.start()
+            later.start()
         pass_on()
         for copy in loads[2:]:
             copy.wait()
@@ -306,7 +303,7 @@
 def finish(gathered, upstream, weight, anchor, first, second, momentum):
     steps, tokens, rows = gathered.shape
     width = upstream.shape[2]
-    block = min(256, rows)
+    block = min(512, rows)
     state = pl.BlockSpec((1, block, width), lambda i: (0, i, 0))
     plain = pl.BlockSpec((block, width), lambda i: (i, 0))
     shape = lambda ref: jax.ShapeDtypeStruct(ref.shape, ref.dtype)

time: 75.5 us -> 75.3 us (level)
  no operation moved by 1% of the time
where the time goes in v4:
time: 75.3 us; the launch traced here: 75.1 us
  Pallas kernels  74.5 us (99%)
    pallas_call x1, Pallas kernels, exchange(): pl.pallas_call(functools.partial(exchange_kernel, n, workers), out_shape=...  69.8 us
    pallas_call x1, Pallas kernels, finish(): pl.pallas_call(finish_kernel, grid=(rows // block,), in_specs=[pl.BlockSp...  4.67 us

profile of v4, /device:TPU:0, one launch (start us, length us, event | category | flops | bytes accessed | tf_op | source)
XLA Modules:
  0.0 75.1 jit_solution(16312874823198246593)
XLA Ops:
  0.6 69.8 %exchange.1 = (bf16[2,512,1024]{2,1,0:T(8,128)(2,1)S(1)}, bf16[2,512,512]{2,1,0:T(8,128)(2,1)S(1)}, f32[1024,512]{1,0:T(8,128)S(1)}, f32[1024,512]{1,0:T(8,128)S...) custom-call(bf16[2,128,4096]{2,1,0:T(8,128)(2,1)} %refs_0_.1, ...), custom_call_target="tpu_custom_call" | custom-call | tf_op jit(solution)/shard_map/exchange/pallas_call | solution.py:240
  70.5 4.7 %finish.1 = (f32[1,1024,512]{2,1,0:T(8,128)}, bf16[1,1024,512]{2,1,0:T(8,128)(2,1)}, bf16[1,1024,512]{2,1,0:T(8,128)(2,1)}, f32[1024,512]{1,0:T(8,128)}, f32[1024,512]{1,0:T(8,128)}) custom-call(bf16[2,512,1024]{2,1,0:T(8,128)(2,1)S(1)} %get-tuple-element.12.x_ref, bf16[2,512,512]{2,1,0:T(8,128)(2,1)S(1)} %get-tuple-element.13.y_ref, ...), custom_call_target="tpu_custom_call" | custom-call | tf_op jit(solution)/shard_map/finish/pallas_call | solution.py:312
